TPU v7x, 32 devices: a whole 2x2x4 slice. The times are simulated.
32 devices in a mesh: blocks: 2 (over x), gz: 8 (over z, y), ta: 2 (over core).
Axes of the slice: x: 2, y: 2, z: 4, core: 2. Of those that a mesh axis runs over, the one named last changes fastest.
Arguments:
- field: float32 [4, 512, 256, 512], P(('blocks', 'ta'), 'gz'), parts along dimension 0, may hold values from -13 to 13
- start_x: float32 [512, 64], replicated, may hold values from -6 to 6
- start_z: float32 [512, 64], replicated, may hold values from -6 to 6
Outputs:
- core: float32 [128, 2, 64, 256], P(('blocks', 'gz'), 'ta'), parts along dimension 0
- basis_x: float32 [1024, 64], P('blocks'), parts along dimension 0
- basis_z: float32 [1024, 64], P('blocks'), parts along dimension 0
There are 2 independent parts, one for each index of `blocks`. A program takes and returns all parts, laid end to end along the dimension named above; an argument that names none is the same for every part. Nothing has to cross between parts.
All inputs are finite; a program needn't handle non-finite values.
Results may differ from a plain program's by a relative error of at most 0.00026.
Values sent between devices are 32-bit elements; how exact they have to be, the bound alone decides.
A program may use at most 128 MiB of HBM per device.

v0:
```python
import jax
import jax.numpy as jnp
from jax import lax
from jax.sharding import PartitionSpec as P

SWEEPS = 3


def orthonormal(block):
    inner = jnp.dot(block.T, block, precision=lax.Precision.HIGHEST)
    lower = jnp.linalg.cholesky(inner)
    return lax.linalg.triangular_solve(lower, block, left_side=False, lower=True, transpose_a=True)


def subspace(make_partial, start):
    basis = start
    gram = lax.psum(make_partial(), ("gz", "ta"))
    for sweep in range(SWEEPS):
        basis = orthonormal(jnp.dot(gram, basis, precision=lax.Precision.HIGHEST))
    return basis


def body(field, start_x, start_z):
    flat = field.reshape(-1, field.shape[3])

    def partial_first():
        return jnp.dot(flat.T, flat, precision=lax.Precision.HIGHEST)

    basis_x = subspace(partial_first, start_x)
    projected = jnp.einsum("tzyx,xr->rtzy", field, basis_x, precision=lax.Precision.HIGHEST)
    rank_slab = lax.all_to_all(projected, "gz", split_axis=0, concat_axis=2, tiled=True)

    def partial_third():
        return jnp.einsum("rtzy,rtwy->zw", rank_slab, rank_slab, precision=lax.Precision.HIGHEST)

    basis_z = subspace(partial_third, start_z)
    core = jnp.einsum("rtzy,zs->rtsy", rank_slab, basis_z, precision=lax.Precision.HIGHEST)
    return (core, basis_x, basis_z)


def solution(mesh):
    in_specs = (P(("blocks", "ta"), "gz", None, None), P(), P())
    out_specs = (P(("blocks", "gz"), "ta", None, None), P("blocks", None), P("blocks", None))
    return jax.shard_map(body, mesh=mesh, in_specs=in_specs, out_specs=out_specs, check_vma=False)
```

profile of v0, /device:TPU:25, one launch (start us, length us, event | category | flops | bytes accessed | tf_op | source)
XLA Modules:
  0.0 504.9 jit_solution(197003309451308451)
XLA Ops:
  7.2 58.8 %fusion.7 = f32[512,512]{1,0:T(8,128)} fusion(f32[1,64,256,512]{3,2,1,0:T(8,128)} %param.6), kind=kOutput, calls=%fused_computation.6 | convolution fusion | flops 51539607552 | bytes 34603008 | tf_op jit(solution)/shard_map/dot_general | solution.py:27
  66.3 91.6 %all-reduce.3.cloned.1.call-done = f32[512,512]{1,0:T(8,128)} async-done(((f32[512,512]{1,0:T(8,128)}), f32[512,512]{1,0:T(8,128)}) %all-reduce.3.cloned.1.call-update) | async-done | bytes 1048592 | tf_op jit(solution)/shard_map/psum | solution.py:17
  157.9 2.4 fusion.42
  160.7 5.8 %cholesky.104 = f32[64,64]{1,0:T(8,128)S(1)} custom-call(f32[64,64]{1,0:T(8,128)S(1)} %fusion.31), custom_call_target="Cholesky" | custom-call | tf_op jit(solution)/shard_map/jit(cholesky)/cholesky | solution.py:11
  167.2 0.7 fusion.12
  167.9 4.9 custom-call.10
  173.1 2.4 fusion.44
  175.8 5.8 %cholesky.115 = f32[64,64]{1,0:T(8,128)S(1)} custom-call(f32[64,64]{1,0:T(8,128)S(1)} %fusion.29), custom_call_target="Cholesky" | custom-call | tf_op jit(solution)/shard_map/jit(cholesky)/cholesky | solution.py:11
  182.4 0.7 fusion.13
  183.0 4.9 custom-call.11
  188.3 1.1 fusion.46
  189.8 5.8 %cholesky.126 = f32[64,64]{1,0:T(8,128)S(1)} custom-call(f32[64,64]{1,0:T(8,128)S(1)} %fusion.27), custom_call_target="Cholesky" | custom-call | tf_op jit(solution)/shard_map/jit(cholesky)/cholesky | solution.py:11
  196.3 0.7 fusion.14
  197.0 4.9 custom-call.12
  202.2 42.2 %fusion.4 = f32[64,1,64,256]{3,0,2,1:T(8,128)} fusion(f32[1,64,256,512]{3,2,1,0:T(8,128)} %param.6, f32[64,512]{1,0:T(8,128)S(1)} %fusion.25), kind=kOutput, calls=%fused_computation.4 | convolution fusion | flops 6442450944 | bytes 37879808 | tf_op jit(solution)/shard_map/tzyx,xr->rtzy/dot_general | solution.py:30
  244.4 4.6 copy.19
  249.0 95.8 %all_to_all.15 = f32[64,1,64,256]{3,2,1,0:T(8,128)S(1)} all-to-all(f32[64,1,64,256]{3,2,1,0:T(8,128)S(1)} %copy.19), channel_id=1, replica_groups=mesh['blocks'=2,'gz'=8,'ta'=2] {'gz'}, dimensions={0} | all-to-all | bytes 8388608 | tf_op jit(solution)/shard_map/all_to_all | solution.py:31
  345.3 1.9 copy-done.1
  347.2 7.9 %convolution_bitcast_fusion = f32[512,512]{1,0:T(8,128)} fusion(f32[8,512,256]{2,1,0:T(8,128)S(1)} %bitcast.130), kind=kOutput, calls=%fused_computation.5 | convolution fusion | flops 6442450944 | bytes 5242880 | tf_op jit(solution)/shard_map/rtzy,rtwy->zw/dot_general | solution.py:34
  355.2 92.6 %all-reduce.5.cloned.1.call-done = f32[512,512]{1,0:T(8,128)} async-done(((f32[512,512]{1,0:T(8,128)}), f32[512,512]{1,0:T(8,128)}) %all-reduce.5.cloned.1.call-update) | async-done | bytes 1048592 | tf_op jit(solution)/shard_map/psum | solution.py:17
  447.8 2.4 fusion.48
  450.6 5.8 %cholesky.137 = f32[64,64]{1,0:T(8,128)S(1)} custom-call(f32[64,64]{1,0:T(8,128)S(1)} %fusion.24), custom_call_target="Cholesky" | custom-call | tf_op jit(solution)/shard_map/jit(cholesky)/cholesky | solution.py:11
  457.1 0.7 fusion.15
  457.8 4.9 custom-call.13
  463.0 2.4 fusion.50
  465.7 6.0 %cholesky.148 = f32[64,64]{1,0:T(8,128)S(1)} custom-call(f32[64,64]{1,0:T(8,128)S(1)} %fusion.22), custom_call_target="Cholesky" | custom-call | tf_op jit(solution)/shard_map/jit(cholesky)/cholesky | solution.py:11
  472.4 0.7 fusion.16
  473.0 4.9 custom-call.14
  478.3 1.1 fusion.52
  479.8 5.8 %cholesky.159 = f32[64,64]{1,0:T(8,128)S(1)} custom-call(f32[64,64]{1,0:T(8,128)S(1)} %fusion.20), custom_call_target="Cholesky" | custom-call | tf_op jit(solution)/shard_map/jit(cholesky)/cholesky | solution.py:11
  487.0 4.9 custom-call.15
  492.2 5.7 %convolution_bitcast_fusion.1 = f32[8,1,64,256]{3,2,1,0:T(8,128)} fusion(f32[8,512,256]{2,1,0:T(8,128)} %bitcast.131, f32[64,512]{1,0:T(8,128)S(1)} %fusion.18), kind=kOutput, calls=%fused_computation.7 | convolution fusion | flops 805306368 | bytes 4849664 | tf_op jit(solution)/shard_map/rtzy,zs->rtsy/dot_general | solution.py:37
  (55 shorter events, 9.6 us)
Async XLA Ops:
  7.2 150.7 %copy-start = (f32[512,64]{0,1:T(8,128)S(1)}, f32[512,64]{0,1:T(8,128)}, u32[]{:S(2)}) copy-start(f32[512,64]{0,1:T(8,128)} %param.7) | copy-start | bytes 393220
  7.2 150.7 %all-reduce.3.cloned.1.call-start = ((), (), s32[]{:S(2)}) async-start(), calls=%async_computation.1 | async-start | bytes 2097152 | tf_op jit(solution)/shard_map/psum | solution.py:17
  66.1 381.7 %all-reduce.5.cloned.1.call-start = ((), (), s32[]{:S(2)}) async-start(), calls=%async_computation.2 | async-start | bytes 2097152 | tf_op jit(solution)/shard_map/psum | solution.py:17
  157.9 30.4 %copy-start.2 = (f32[512,512]{1,0:T(8,128)S(1)}, f32[512,512]{1,0:T(8,128)}, u32[]{:S(2)}) copy-start(f32[512,512]{1,0:T(8,128)} %all-reduce.3.cloned.1.call-done) | copy-start | bytes 3145732
  202.2 42.2 %copy-start.4 = (f32[64,512]{1,0:T(8,128)}, f32[64,512]{1,0:T(8,128)S(1)}, u32[]{:S(2)}) copy-start(f32[64,512]{1,0:T(8,128)S(1)} %fusion.25) | copy-start | bytes 393220
  345.3 1.9 copy-start.1
  347.2 100.5 %copy-start.6 = (f32[512,64]{0,1:T(8,128)S(1)}, f32[512,64]{0,1:T(8,128)}, u32[]{:S(2)}) copy-start(f32[512,64]{0,1:T(8,128)} %param.8) | copy-start | bytes 393220
  447.8 30.5 %copy-start.3 = (f32[512,512]{1,0:T(8,128)S(1)}, f32[512,512]{1,0:T(8,128)}, u32[]{:S(2)}) copy-start(f32[512,512]{1,0:T(8,128)} %all-reduce.5.cloned.1.call-done) | copy-start | bytes 3145732
  492.2 5.7 %copy-start.5 = (f32[64,512]{1,0:T(8,128)}, f32[64,512]{1,0:T(8,128)S(1)}, u32[]{:S(2)}) copy-start(f32[64,512]{1,0:T(8,128)S(1)} %fusion.18) | copy-start | bytes 393220
Sparse Core Ops, SparseCore 0:
  66.2 91.6 all-reduce.2
  355.3 92.4 all-reduce.4
where the time goes:
time: 515 us; the launch traced here: 505 us
  waiting for transfers between devices  184 us (36%)
  matrix products  130 us (25%)
  blocking collectives  95.8 us (19%)
  other arithmetic  72.6 us (14%)
  between operations  14.5 us (3%)
  local copies, waits for them, and re-layouts  7.51 us (1%)
    psum x2, waiting for transfers between devices, subspace(): gram = lax.psum(make_partial(), ('gz', 'ta'))  184 us
    all_to_all x1, blocking collectives, body(): lax.all_to_all(projected, 'gz', split_axis=0, concat_axis=2, tiled=True)  95.8 us
    dot_general x1, matrix products, partial_first(): return jnp.dot(flat.T, flat, precision=lax.Precision.HIGHEST)  58.8 us
    dot_general x1, matrix products, body(): jnp.einsum('tzyx,xr->rtzy', field, basis_x, precision=lax.Precision.HIGHEST)  42.2 us
    another operation x18, other arithmetic, orthonormal(): lower = jnp.linalg.cholesky(inner)  39.2 us
    another operation x12, other arithmetic, orthonormal(): lax.linalg.triangular_solve(lower, block, left_side=False, lower=True, tr...  33.3 us
    dot_general x6, matrix products, subspace(): basis = orthonormal(jnp.dot(gram, basis, precision=lax.Precision.HIGHEST))  11.9 us
  transfers between devices with their start and end apart: 2, of which 2 were waited for; matrix products, arithmetic and copies ran while one was open for 0% of the time, Pallas kernels for 0%

commit v1 on v0

v1 whole, which is shorter than its diff:
```python
import functools

import jax
import jax.numpy as jnp
from jax import lax
from jax.experimental import pallas as pl
from jax.experimental.pallas import tpu as pltpu
from jax.sharding import PartitionSpec as P

SWEEPS = 3
LANES = 128
MESH = pl.DeviceIdType.MESH
VMEM = pl.BlockSpec(memory_space=pltpu.VMEM)
LIMIT = 56 * 2**20


def params(**more):
    return pltpu.CompilerParams(vmem_limit_bytes=LIMIT, **more)


def split(x):
    high = x.astype(jnp.bfloat16)
    return high, (x - high.astype(jnp.float32)).astype(jnp.bfloat16)


def add_products(x, axis, sums):
    high, low = split(x)
    dims = (((axis,), (axis,)), ((), ()))
    sums[...] += lax.dot_general(
        high, jnp.concatenate([high, low], axis=1 - axis), dims, preferred_element_type=jnp.float32
    )


def pack(sums, out_ref):
    size = sums.shape[0]
    start = 0
    for block in range(size // LANES):
        first, depth = block * LANES, size - block * LANES
        columns, rows = pl.ds(first, LANES), pl.ds(first, depth)
        cross = sums[rows, pl.ds(size + first, LANES)] + sums[columns, pl.ds(size + first, depth)].T
        out_ref[pl.ds(start, depth), :] = sums[rows, columns] + cross
        start += depth
    if start < out_ref.shape[0]:
        out_ref[pl.ds(start, out_ref.shape[0] - start), :] = jnp.zeros((out_ref.shape[0] - start, LANES), jnp.float32)


def gram_kernel(axis, x_ref, out_ref, sums):
    @pl.when(pl.program_id(0) == 0)
    def _():
        sums[...] = jnp.zeros_like(sums)

    add_products(x_ref[...] if axis == 0 else x_ref[0], axis, sums)

    @pl.when(pl.program_id(0) == pl.num_programs(0) - 1)
    def _():
        pack(sums, out_ref)


def packed_rows(size, n):
    blocks = size // LANES
    rows = LANES * blocks * (blocks + 1) // 2
    unit = 16 * n
    return -(-rows // unit) * unit


def gram(x, axis, rows):
    size = x.shape[1]
    if axis == 0:
        step = min(1024, x.shape[0])
        grid, spec = x.shape[0] // step, pl.BlockSpec((step, size), lambda i: (i, 0))
    else:
        grid, spec = x.shape[0], pl.BlockSpec((1,) + x.shape[1:], lambda i: (i, 0, 0))
    return pl.pallas_call(
        functools.partial(gram_kernel, axis),
        grid=(grid,),
        in_specs=[spec],
        out_specs=pl.BlockSpec((rows, LANES), lambda i: (0, 0)),
        out_shape=jax.ShapeDtypeStruct((rows, LANES), jnp.float32),
        scratch_shapes=[pltpu.VMEM((size, 2 * size), jnp.float32)],
        compiler_params=params(),
    )(x)


def total_kernel(n, x_ref, out_ref, other, half, parts, pair, scatter, collect, back):
    g, c = lax.axis_index("gz"), lax.axis_index("ta")
    mate = {"ta": 1 - c}
    piece = parts.shape[1]
    depth = n * piece
    mine = pl.multiple_of(c * depth, 8)
    theirs = pl.multiple_of((1 - c) * depth, 8)

    def rows(base, k):
        return pl.ds(pl.multiple_of(base + k * piece, 8), piece)

    barrier = pltpu.get_barrier_semaphore()
    pl.semaphore_signal(barrier, inc=1, device_id=mate, device_id_type=MESH)

    @pl.loop(1, n)
    def _(i):
        pl.semaphore_signal(barrier, inc=1, device_id={"gz": lax.rem(g + i, n)}, device_id_type=MESH)

    pl.semaphore_wait(barrier, n)

    first = pltpu.make_async_remote_copy(
        x_ref.at[pl.ds(theirs, depth)], other, pair.at[0], pair.at[1], device_id=mate, device_id_type=MESH
    )
    first.start()
    first.wait()
    half[...] = x_ref[pl.ds(mine, depth), :] + other[...]

    def send(i):
        k = lax.rem(g + i, n)
        return pltpu.make_async_remote_copy(
            half.at[rows(0, k)], parts.at[i - 1], scatter.at[0, i], scatter.at[1, i], device_id={"gz": k}, device_id_type=MESH
        )

    def publish(i):
        k = lax.rem(g + i, n)
        own = out_ref.at[rows(mine, g)]
        return pltpu.make_async_remote_copy(
            own, own, collect.at[0, i], collect.at[1, i], device_id={"gz": k}, device_id_type=MESH
        )

    def forward(i):
        own = out_ref.at[rows(mine, lax.rem(g + n - i, n))]
        return pltpu.make_async_remote_copy(own, own, back.at[0, i], back.at[1, i], device_id=mate, device_id_type=MESH)

    @pl.loop(1, n)
    def _(i):
        send(i).start()

    @pl.loop(1, n)
    def _(i):
        send(i).wait_recv()

    out_ref[rows(mine, g), :] = half[rows(0, g), :] + jnp.sum(parts[...], axis=0)

    @pl.loop(1, n)
    def _(i):
        publish(i).start()

    forward(0).start()

    @pl.loop(1, n)
    def _(i):
        publish(i).wait_recv()
        forward(i).start()

    @pl.loop(0, n)
    def _(i):
        forward(i).wait()

    @pl.loop(1, n)
    def _(i):
        send(i).wait_send()
        publish(i).wait_send()


def total(x, n, collective_id):
    piece = x.shape[0] // (2 * n)
    dma = pltpu.SemaphoreType.DMA
    return pl.pallas_call(
        functools.partial(total_kernel, n),
        in_specs=[VMEM],
        out_specs=VMEM,
        out_shape=jax.ShapeDtypeStruct(x.shape, x.dtype),
        scratch_shapes=[
            pltpu.VMEM((n * piece, LANES), x.dtype),
            pltpu.VMEM((n * piece, LANES), x.dtype),
            pltpu.VMEM((n - 1, piece, LANES), x.dtype),
            dma((2,)),
            dma((2, n)),
            dma((2, n)),
            dma((2, n)),
        ],
        compiler_params=params(collective_id=collective_id, has_side_effects=True),
    )(x)


def exact(a, b, contract):
    return lax.dot_general(
        a, b, ((contract[:1], contract[1:]), ((), ())), precision=lax.Precision.HIGHEST, preferred_element_type=jnp.float32
    )


def inverse_factor(inner):
    r = inner.shape[0]
    row_id = lax.broadcasted_iota(jnp.int32, (r, 1), 0)
    eye = (lax.broadcasted_iota(jnp.int32, (r, r), 0) == lax.broadcasted_iota(jnp.int32, (r, r), 1)).astype(jnp.float32)
    work = jnp.concatenate([inner, eye], axis=1)
    tiles = [work[8 * t : 8 * t + 8] for t in range(r // 8)]
    local = lax.broadcasted_iota(jnp.int32, (8, 1), 0)
    for j in range(r):
        t0, s = divmod(j, 8)
        row = tiles[t0][s : s + 1]
        scaled = row * (1.0 / row[:, j : j + 1])
        if s < 7:
            factor = jnp.where(local > s, tiles[t0][:, j : j + 1], 0.0)
            updated = tiles[t0] - factor * scaled
        else:
            updated = tiles[t0]
        for t in range(t0 + 1, r // 8):
            tiles[t] = tiles[t] - tiles[t][:, j : j + 1] * scaled
        tiles[t0] = updated
    work = jnp.concatenate(tiles, axis=0)
    pivots = jnp.sum(work[:, :r] * eye, axis=1, keepdims=True)
    return work[:, r:] * (1.0 / jnp.sqrt(pivots))


def sweeps_kernel(g_ref, q_ref, out_ref, full):
    size = full.shape[0]
    start = 0
    for block in range(size // LANES):
        columns = pl.ds(block * LANES, LANES)
        full[pl.ds(block * LANES, size - block * LANES), columns] = g_ref[pl.ds(start, size - block * LANES), :]
        if block * LANES + LANES < size:
            below = pl.ds(block * LANES + LANES, size - block * LANES - LANES)
            full[columns, below] = g_ref[pl.ds(start + LANES, size - block * LANES - LANES), :].T
        start += size - block * LANES
    q = q_ref[...]
    for sweep in range(SWEEPS):
        z = exact(q, full[...], (1, 0))
        q = exact(inverse_factor(exact(z, z, (1, 1))), z, (1, 0))
    out_ref[...] = q


def subspace(packed, start_t):
    size = start_t.shape[1]
    return pl.pallas_call(
        sweeps_kernel,
        in_specs=[VMEM, VMEM],
        out_specs=VMEM,
        out_shape=jax.ShapeDtypeStruct(start_t.shape, jnp.float32),
        scratch_shapes=[pltpu.VMEM((size, size), jnp.float32)],
        compiler_params=params(),
    )(packed, start_t)


def body(n, field, start_x, start_z):
    flat = field.reshape(-1, field.shape[3])
    basis_x = subspace(total(gram(flat, 0, packed_rows(flat.shape[1], n)), n, 0), start_x.T)
    projected = jnp.einsum("tzyx,rx->rtzy", field, basis_x, precision=lax.Precision.HIGH)
    slab = lax.all_to_all(projected, "gz", split_axis=0, concat_axis=2, tiled=True)
    flat_slab = slab.reshape((-1,) + slab.shape[2:])
    basis_z = subspace(total(gram(flat_slab, 1, packed_rows(slab.shape[2], n)), n, 1), start_z.T)
    core = jnp.einsum("rtzy,sz->rtsy", slab, basis_z, precision=lax.Precision.HIGH)
    return (core, basis_x.T, basis_z.T)


def solution(mesh):
    in_specs = (P(("blocks", "ta"), "gz", None, None), P(), P())
    out_specs = (P(("blocks", "gz"), "ta", None, None), P("blocks", None), P("blocks", None))
    return jax.shard_map(
        functools.partial(body, mesh.shape["gz"]), mesh=mesh, in_specs=in_specs, out_specs=out_specs, check_vma=False
    )
```

time: 515 us -> 260 us (0.50); the launches traced: 505 us -> 259 us
  waiting for transfers between devices: 184 us -> 0 us
  Pallas kernels: 0 us -> 131 us
  matrix products: 130 us -> 25.7 us
  other arithmetic: 72.6 us -> 0 us
  between operations: 14.5 us -> 0.65 us
    psum x2 -> x0, waiting for transfers between devices: 184 us -> none  [subspace(): gram = lax.psum(make_partial(), ('gz', 'ta'))]
    pallas_call x0 -> x6, Pallas kernels: none -> 131 us  [the longest x2 54.2 us: total(): pl.pallas_call(functools.partial(total_kernel, n), in_specs=[VMEM], out_s...]
    dot_general x16 -> x2, matrix products: 128 us -> 25.7 us  [the longest x1 22.5 us: body(): jnp.einsum('tzyx,rx->rtzy', field, basis_x, precision=lax.Precision.HIGH)]
    another operation x30 -> x0, other arithmetic: 72.5 us -> none  [the longest x18 39.2 us: orthonormal(): lower = jnp.linalg.cholesky(inner)]
  transfers between devices with their start and end apart: 2 -> 0, of which waited for: 2 -> 0; matrix products, arithmetic and copies ran while one was open for 0% -> 0% of each run, Pallas kernels for 0% -> 0%
where the time goes in v1:
time: 260 us; the launch traced here: 259 us
  Pallas kernels  131 us (50%)
  blocking collectives  95.4 us (37%)
  matrix products  25.7 us (10%)
  local copies, waits for them, and re-layouts  6.86 us (3%)
    all_to_all x1, blocking collectives, body(): lax.all_to_all(projected, 'gz', split_axis=0, concat_axis=2, tiled=True)  95.4 us
    pallas_call x2, Pallas kernels, total(): pl.pallas_call(functools.partial(total_kernel, n), in_specs=[VMEM], out_s...  54.2 us
    pallas_call x2, Pallas kernels, subspace(): pl.pallas_call(sweeps_kernel, in_specs=[VMEM, VMEM], out_specs=VMEM, out_...  42.4 us
    pallas_call x2, Pallas kernels, gram(): pl.pallas_call(functools.partial(gram_kernel, axis), grid=(grid,), in_spe...  34.1 us
    dot_general x1, matrix products, body(): jnp.einsum('tzyx,rx->rtzy', field, basis_x, precision=lax.Precision.HIGH)  22.5 us

profile of v1, /device:TPU:25, one launch (start us, length us, event | category | flops | bytes accessed | tf_op | source)
XLA Modules:
  0.0 259.4 jit_solution(14018879746688408422)
XLA Ops:
  0.6 26.0 %shard_map.58.x_ref = f32[1280,128]{1,0:T(8,128)} custom-call(f32[16384,512]{1,0:T(8,128)} %bitcast.29), custom_call_target="tpu_custom_call" | custom-call | tf_op jit(solution)/shard_map/pallas_call | solution.py:73
  26.6 26.5 %shard_map.59.g_ref = f32[1280,128]{1,0:T(8,128)} custom-call(f32[1280,128]{1,0:T(8,128)} %shard_map.58.x_ref), custom_call_target="tpu_custom_call" | custom-call | tf_op jit(solution)/shard_map/pallas_call | solution.py:162
  53.1 21.2 %shard_map.60 = f32[64,512]{1,0:T(8,128)} custom-call(f32[1280,128]{1,0:T(8,128)} %shard_map.59.g_ref, f32[64,512]{1,0:T(8,128)} %bitcast.35), custom_call_target="tpu_custom_call" | custom-call | tf_op jit(solution)/shard_map/pallas_call | solution.py:229
  74.3 22.5 %fusion.2 = f32[64,1,64,256]{3,0,2,1:T(8,128)} fusion(f32[1,64,256,512]{3,2,1,0:T(8,128)} %param.3, f32[64,512]{1,0:T(8,128)} %shard_map.60), kind=kOutput, calls=%fused_computation.2 | convolution fusion | flops 3221225472 | bytes 37879808 | tf_op jit(solution)/shard_map/tzyx,rx->rtzy/dot_general | solution.py:242
  96.8 4.6 %copy.8 = f32[64,1,64,256]{3,2,1,0:T(8,128)S(1)} copy(f32[64,1,64,256]{3,0,2,1:T(8,128)} %fusion.2) | data formatting | bytes 8388608 | tf_op jit(solution)/shard_map/tzyx,rx->rtzy/dot_general | solution.py:242
  101.5 95.4 %all_to_all.15 = f32[64,1,64,256]{3,2,1,0:T(8,128)S(1)} all-to-all(f32[64,1,64,256]{3,2,1,0:T(8,128)S(1)} %copy.8), channel_id=1, replica_groups=mesh['blocks'=2,'gz'=8,'ta'=2] {'gz'}, dimensions={0} | all-to-all | bytes 8388608 | tf_op jit(solution)/shard_map/all_to_all | solution.py:243
  196.9 2.2 copy.9
  199.1 0.0 copy-start
  199.1 8.1 %shard_map.61.x_ref = f32[1280,128]{1,0:T(8,128)} custom-call(f32[8,512,256]{2,1,0:T(8,128)} %bitcast.30), custom_call_target="tpu_custom_call" | custom-call | tf_op jit(solution)/shard_map/pallas_call | solution.py:73
  207.2 27.7 %shard_map.62.g_ref = f32[1280,128]{1,0:T(8,128)} custom-call(f32[1280,128]{1,0:T(8,128)} %shard_map.61.x_ref), custom_call_target="tpu_custom_call" | custom-call | tf_op jit(solution)/shard_map/pallas_call | solution.py:162
  234.9 21.2 %shard_map.63 = f32[64,512]{1,0:T(8,128)} custom-call(f32[1280,128]{1,0:T(8,128)} %shard_map.62.g_ref, f32[64,512]{1,0:T(8,128)} %bitcast.36), custom_call_target="tpu_custom_call" | custom-call | tf_op jit(solution)/shard_map/pallas_call | solution.py:229
  256.2 0.0 copy-done
  256.2 3.2 %convolution_bitcast_fusion = f32[8,1,64,256]{3,2,1,0:T(8,128)} fusion(f32[8,512,256]{2,1,0:T(8,128)S(1)} %bitcast.31, f32[64,512]{1,0:T(8,128)} %shard_map.63), kind=kOutput, calls=%fused_computation.3 | convolution fusion | flops 402653184 | bytes 4849664 | tf_op jit(solution)/shard_map/rtzy,sz->rtsy/dot_general | solution.py:246
Async XLA Ops:
  199.1 57.1 %copy-start = (f32[8,8,1,64,256]{4,3,0,1,2:T(8,128)S(1)}, f32[8,8,1,64,256]{4,3,0,1,2:T(8,128)}, u32[]{:S(2)}) copy-start(f32[8,8,1,64,256]{4,3,0,1,2:T(8,128)} %copy.9) | copy-start | bytes 12582916

commit v2 on v1

--- a/solution.py
+++ b/solution.py
@@ -236,14 +236,125 @@
     )(packed, start_t)
 
 
+def shuffle_kernel(n, field, w_ref, slab, packed, sent, chunks, sums, load, send_sem, recv_sem):
+    g = lax.axis_index("gz")
+    rank, depth = slab.shape[0], sent.shape[1]
+    planes = chunks.shape[1]
+    groups = depth // planes
+    count = groups * (slab.shape[2] // LANES)
+    at = pl.multiple_of(g * depth, 8)
+
+    def place(c):
+        plane = pl.multiple_of(lax.rem(c, groups) * planes, 8)
+        return plane, pl.ds(pl.multiple_of(lax.div(c, groups) * LANES, LANES), LANES)
+
+    def fetch(c):
+        plane, columns = place(c)
+        slot = lax.rem(c, 2)
+        return pltpu.make_async_copy(field.at[pl.ds(plane, planes), columns, :], chunks.at[slot], load.at[slot])
+
+    def ship(i, source, target, columns, half):
+        k = lax.rem(g + i, n)
+        return pltpu.make_async_remote_copy(
+            sent.at[pl.ds(k * rank, rank), source, columns],
+            slab.at[:, target, columns],
+            send_sem.at[half, i],
+            recv_sem.at[half, i],
+            device_id={"gz": k},
+            device_id_type=MESH,
+        )
+
+    fetch(0).start()
+    barrier = pltpu.get_barrier_semaphore()
+
+    @pl.loop(1, n)
+    def _(i):
+        pl.semaphore_signal(barrier, inc=1, device_id={"gz": lax.rem(g + i, n)}, device_id_type=MESH)
+
+    w_high, w_low = split(w_ref[...])
+    both = jnp.concatenate([w_high, w_low], axis=0)
+    r = w_high.shape[0]
+    dims = (((1,), (1,)), ((), ()))
+    sums[...] = jnp.zeros_like(sums)
+    pl.semaphore_wait(barrier, n - 1)
+
+    @pl.loop(0, count)
+    def _(c):
+        @pl.when(c + 1 < count)
+        def _():
+            fetch(c + 1).start()
+
+        fetch(c).wait()
+        plane, columns = place(c)
+        high, low = split(chunks[lax.rem(c, 2)].reshape(planes * LANES, chunks.shape[3]))
+        first = lax.dot_general(both, high, dims, preferred_element_type=jnp.float32)
+        second = lax.dot_general(w_high, low, dims, preferred_element_type=jnp.float32)
+        sent[:, pl.ds(plane, planes), columns] = (first[:r] + first[r:] + second).reshape(r, planes, LANES)
+
+        @pl.loop(1, n)
+        def _(i):
+            ship(
+                i, pl.ds(plane, planes), pl.ds(pl.multiple_of(at + plane, 8), planes), columns, lax.div(c, groups)
+            ).start()
+
+    slab[:, pl.ds(at, depth), :] = sent[pl.ds(g * rank, rank)]
+
+    @pl.loop(0, slab.shape[2] // LANES)
+    def _(half):
+        columns = pl.ds(pl.multiple_of(half * LANES, LANES), LANES)
+
+        @pl.loop(1, n)
+        def _(i):
+            k = lax.rem(g + n - i, n)
+            ship(i, pl.ds(0, depth), pl.ds(pl.multiple_of(k * depth, 8), depth), columns, half).wait_recv()
+
+        @pl.loop(0, rank // 2)
+        def _(pair):
+            x = jnp.concatenate([slab[2 * pair, :, columns], slab[2 * pair + 1, :, columns]], axis=1)
+            add_products(x, 1, sums)
+
+    pack(sums, packed)
+
+    @pl.loop(0, slab.shape[2] // LANES)
+    def _(half):
+        columns = pl.ds(pl.multiple_of(half * LANES, LANES), LANES)
+
+        @pl.loop(1, n)
+        def _(i):
+            ship(i, pl.ds(0, depth), pl.ds(at, depth), columns, half).wait_send()
+
+
+def shuffle(field, w, n, collective_id):
+    depth, width, cells = field.shape
+    r, size = w.shape[0], depth * n
+    rows = packed_rows(size, n)
+    dma = pltpu.SemaphoreType.DMA
+    return pl.pallas_call(
+        functools.partial(shuffle_kernel, n),
+        in_specs=[pl.BlockSpec(memory_space=pl.ANY), VMEM],
+        out_specs=[VMEM, VMEM],
+        out_shape=[
+            jax.ShapeDtypeStruct((r // n, size, width), jnp.float32),
+            jax.ShapeDtypeStruct((rows, LANES), jnp.float32),
+        ],
+        scratch_shapes=[
+            pltpu.VMEM((r, depth, width), jnp.float32),
+            pltpu.VMEM((2, 8, LANES, cells), jnp.float32),
+            pltpu.VMEM((size, 2 * size), jnp.float32),
+            dma((2,)),
+            dma((width // LANES, n)),
+            dma((width // LANES, n)),
+        ],
+        compiler_params=params(collective_id=collective_id, has_side_effects=True),
+    )(field, w)
+
+
 def body(n, field, start_x, start_z):
     flat = field.reshape(-1, field.shape[3])
     basis_x = subspace(total(gram(flat, 0, packed_rows(flat.shape[1], n)), n, 0), start_x.T)
-    projected = jnp.einsum("tzyx,rx->rtzy", field, basis_x, precision=lax.Precision.HIGH)
-    slab = lax.all_to_all(projected, "gz", split_axis=0, concat_axis=2, tiled=True)
-    flat_slab = slab.reshape((-1,) + slab.shape[2:])
-    basis_z = subspace(total(gram(flat_slab, 1, packed_rows(slab.shape[2], n)), n, 1), start_z.T)
-    core = jnp.einsum("rtzy,sz->rtsy", slab, basis_z, precision=lax.Precision.HIGH)
+    slab, packed = shuffle(field[0], basis_x, n, 2)
+    basis_z = subspace(total(packed, n, 1), start_z.T)
+    core = jnp.einsum("rzy,sz->rsy", slab, basis_z, precision=lax.Precision.HIGH)[:, None]
     return (core, basis_x.T, basis_z.T)
 
 

time: 260 us -> 227 us (0.87)
  blocking collectives: 95.4 us -> 0 us
  Pallas kernels: 131 us -> 221 us
  matrix products: 25.7 us -> 4.5 us
  local copies, waits for them, and re-layouts: 6.86 us -> 0 us
    pallas_call x0 -> x1, Pallas kernels: none -> 99.3 us  [shuffle(): pl.pallas_call(functools.partial(shuffle_kernel, n), in_specs=[pl.BlockSp...]
    all_to_all x1 -> x0, blocking collectives: 95.4 us -> none  [body(): lax.all_to_all(projected, 'gz', split_axis=0, concat_axis=2, tiled=True)]
    dot_general x2 -> x1, matrix products: 25.7 us -> 4.5 us  [body(): jnp.einsum('rzy,sz->rsy', slab, basis_z, precision=lax.Precision.HIGH)]
    pallas_call x2 -> x1, Pallas kernels: 34.1 us -> 26 us  [gram(): pl.pallas_call(functools.partial(gram_kernel, axis), grid=(grid,), in_spe...]
    dot_general x1 -> x0, local copies, waits for them, and re-layouts: 4.62 us -> none  [body(): jnp.einsum('tzyx,rx->rtzy', field, basis_x, precision=lax.Precision.HIGH)]
where the time goes in v2:
time: 227 us; the launch traced here: 226 us
  Pallas kernels  221 us (97%)
  matrix products  4.5 us (2%)
    pallas_call x1, Pallas kernels, shuffle(): pl.pallas_call(functools.partial(shuffle_kernel, n), in_specs=[pl.BlockSp...  99.3 us
    pallas_call x2, Pallas kernels, total(): pl.pallas_call(functools.partial(total_kernel, n), in_specs=[VMEM], out_s...  53.6 us
    pallas_call x2, Pallas kernels, subspace(): pl.pallas_call(sweeps_kernel, in_specs=[VMEM, VMEM], out_specs=VMEM, out_...  42.4 us
    pallas_call x1, Pallas kernels, gram(): pl.pallas_call(functools.partial(gram_kernel, axis), grid=(grid,), in_spe...  26 us

profile of v2, /device:TPU:25, one launch (start us, length us, event | category | flops | bytes accessed | tf_op | source)
XLA Modules:
  0.0 226.5 jit_solution(6023411982237006654)
XLA Ops:
  0.6 26.0 %shard_map.58.x_ref = f32[1280,128]{1,0:T(8,128)} custom-call(f32[16384,512]{1,0:T(8,128)} %bitcast.16), custom_call_target="tpu_custom_call" | custom-call | tf_op jit(solution)/shard_map/pallas_call | solution.py:73
  26.6 26.5 %shard_map.59.g_ref = f32[1280,128]{1,0:T(8,128)} custom-call(f32[1280,128]{1,0:T(8,128)} %shard_map.58.x_ref), custom_call_target="tpu_custom_call" | custom-call | tf_op jit(solution)/shard_map/pallas_call | solution.py:162
  53.1 21.2 %shard_map.60.w_ref = f32[64,512]{1,0:T(8,128)} custom-call(f32[1280,128]{1,0:T(8,128)} %shard_map.59.g_ref, f32[64,512]{1,0:T(8,128)} %bitcast.20), custom_call_target="tpu_custom_call" | custom-call | tf_op jit(solution)/shard_map/pallas_call | solution.py:229
  74.3 99.3 %shard_map.61 = (f32[8,512,256]{2,1,0:T(8,128)}, f32[1280,128]{1,0:T(8,128)}) custom-call(f32[64,256,512]{2,1,0:T(8,128)} %bitcast.17, f32[64,512]{1,0:T(8,128)} %shard_map.60.w_ref), custom_call_target="tpu_custom_call" | custom-call | tf_op jit(solution)/shard_map/pallas_call | solution.py:332
  173.6 27.1 %shard_map.62.g_ref = f32[1280,128]{1,0:T(8,128)} custom-call(f32[1280,128]{1,0:T(8,128)} %get-tuple-element.5.x_ref), custom_call_target="tpu_custom_call" | custom-call | tf_op jit(solution)/shard_map/pallas_call | solution.py:162
  200.8 21.2 %shard_map.63 = f32[64,512]{1,0:T(8,128)} custom-call(f32[1280,128]{1,0:T(8,128)} %shard_map.62.g_ref, f32[64,512]{1,0:T(8,128)} %bitcast.21), custom_call_target="tpu_custom_call" | custom-call | tf_op jit(solution)/shard_map/pallas_call | solution.py:229
  222.0 4.5 %convolution_bitcast_fusion = f32[8,1,64,256]{3,2,1,0:T(8,128)} fusion(f32[8,512,256]{2,1,0:T(8,128)} %get-tuple-element.6, f32[64,512]{1,0:T(8,128)} %shard_map.63), kind=kOutput, calls=%fused_computation | convolution fusion | flops 402653184 | bytes 4849664 | tf_op jit(solution)/shard_map/rzy,sz->rsy/dot_general | solution.py:357

commit v3 on v2

--- a/solution.py
+++ b/solution.py
@@ -9,6 +9,7 @@
 
 SWEEPS = 3
 LANES = 128
+STEP = 8
 MESH = pl.DeviceIdType.MESH
 VMEM = pl.BlockSpec(memory_space=pltpu.VMEM)
 LIMIT = 56 * 2**20
@@ -66,7 +67,7 @@
 def gram(x, axis, rows):
     size = x.shape[1]
     if axis == 0:
-        step = min(1024, x.shape[0])
+        step = min(2048, x.shape[0])
         grid, spec = x.shape[0] // step, pl.BlockSpec((step, size), lambda i: (i, 0))
     else:
         grid, spec = x.shape[0], pl.BlockSpec((1,) + x.shape[1:], lambda i: (i, 0, 0))
@@ -190,18 +191,30 @@
     work = jnp.concatenate([inner, eye], axis=1)
     tiles = [work[8 * t : 8 * t + 8] for t in range(r // 8)]
     local = lax.broadcasted_iota(jnp.int32, (8, 1), 0)
-    for j in range(r):
+    def spread(x):
+        return jnp.broadcast_to(x, (8, 2 * r))
+
+    for j in range(0, r, STEP):
         t0, s = divmod(j, 8)
-        row = tiles[t0][s : s + 1]
-        scaled = row * (1.0 / row[:, j : j + 1])
-        if s < 7:
-            factor = jnp.where(local > s, tiles[t0][:, j : j + 1], 0.0)
-            updated = tiles[t0] - factor * scaled
-        else:
-            updated = tiles[t0]
-        for t in range(t0 + 1, r // 8):
-            tiles[t] = tiles[t] - tiles[t][:, j : j + 1] * scaled
-        tiles[t0] = updated
+        upper = [[spread(tiles[t0][s + k : s + k + 1, j + m : j + m + 1]) for m in range(STEP)] for k in range(STEP)]
+        rows = [spread(tiles[t0][s + k : s + k + 1]) for k in range(STEP)]
+        columns = [[spread(tile[:, j + k : j + k + 1]) for k in range(STEP)] for tile in tiles[t0:]]
+        inverse, ratio = [], []
+        for k in range(STEP):
+            inverse.append(1.0 / upper[k][k])
+            ratio.append([upper[k][m] * inverse[k] for m in range(STEP)])
+            for q in range(k + 1, STEP):
+                rows[q] = rows[q] - ratio[k][q] * rows[k]
+                for m in range(q, STEP):
+                    upper[q][m] = upper[q][m] - ratio[k][q] * upper[k][m]
+        scaled = [rows[k] * inverse[k] for k in range(STEP)]
+        for t in range(t0, r // 8):
+            own = columns[t - t0]
+            for k in range(STEP):
+                for q in range(k + 1, STEP):
+                    own[q] = own[q] - own[k] * ratio[k][q]
+                factor = jnp.where(local > s + k, own[k], 0.0) if t == t0 else own[k]
+                tiles[t] = tiles[t] - factor * scaled[k]
     work = jnp.concatenate(tiles, axis=0)
     pivots = jnp.sum(work[:, :r] * eye, axis=1, keepdims=True)
     return work[:, r:] * (1.0 / jnp.sqrt(pivots))

time: 227 us -> 203 us (0.89)
  Pallas kernels: 221 us -> 198 us
    pallas_call x2, Pallas kernels: 42.4 us -> 22.2 us  [subspace(): pl.pallas_call(sweeps_kernel, in_specs=[VMEM, VMEM], out_specs=VMEM, out_...]
    pallas_call x1, Pallas kernels: 26 us -> 22.5 us  [gram(): pl.pallas_call(functools.partial(gram_kernel, axis), grid=(grid,), in_spe...]
where the time goes in v3:
time: 203 us
  Pallas kernels  198 us (98%)
  matrix products  4.49 us (2%)
    pallas_call x1, Pallas kernels, shuffle(): pl.pallas_call(functools.partial(shuffle_kernel, n), in_specs=[pl.BlockSp...  99.3 us
    pallas_call x2, Pallas kernels, total(): pl.pallas_call(functools.partial(total_kernel, n), in_specs=[VMEM], out_s...  53.6 us
    pallas_call x1, Pallas kernels, gram(): pl.pallas_call(functools.partial(gram_kernel, axis), grid=(grid,), in_spe...  22.5 us
    pallas_call x2, Pallas kernels, subspace(): pl.pallas_call(sweeps_kernel, in_specs=[VMEM, VMEM], out_specs=VMEM, out_...  22.2 us
    dot_general x1, matrix products, body(): jnp.einsum('rzy,sz->rsy', slab, basis_z, precision=lax.Precision.HIGH)  4.49 us

profile of v3, /device:TPU:25, one launch (start us, length us, event | category | flops | bytes accessed | tf_op | source)
XLA Modules:
  0.0 202.7 jit_solution(4174441432447431582)
XLA Ops:
  0.6 22.5 %shard_map.58.x_ref = f32[1280,128]{1,0:T(8,128)} custom-call(f32[16384,512]{1,0:T(8,128)} %bitcast.16), custom_call_target="tpu_custom_call" | custom-call | tf_op jit(solution)/shard_map/pallas_call | solution.py:74
  23.1 26.5 %shard_map.59.g_ref = f32[1280,128]{1,0:T(8,128)} custom-call(f32[1280,128]{1,0:T(8,128)} %shard_map.58.x_ref), custom_call_target="tpu_custom_call" | custom-call | tf_op jit(solution)/shard_map/pallas_call | solution.py:163
  49.6 11.1 %shard_map.60.w_ref = f32[64,512]{1,0:T(8,128)} custom-call(f32[1280,128]{1,0:T(8,128)} %shard_map.59.g_ref, f32[64,512]{1,0:T(8,128)} %bitcast.20), custom_call_target="tpu_custom_call" | custom-call | tf_op jit(solution)/shard_map/pallas_call | solution.py:242
  60.7 99.3 %shard_map.61 = (f32[8,512,256]{2,1,0:T(8,128)}, f32[1280,128]{1,0:T(8,128)}) custom-call(f32[64,256,512]{2,1,0:T(8,128)} %bitcast.17, f32[64,512]{1,0:T(8,128)} %shard_map.60.w_ref), custom_call_target="tpu_custom_call" | custom-call | tf_op jit(solution)/shard_map/pallas_call | solution.py:345
  160.0 27.1 %shard_map.62.g_ref = f32[1280,128]{1,0:T(8,128)} custom-call(f32[1280,128]{1,0:T(8,128)} %get-tuple-element.5.x_ref), custom_call_target="tpu_custom_call" | custom-call | tf_op jit(solution)/shard_map/pallas_call | solution.py:163
  187.1 11.1 %shard_map.63 = f32[64,512]{1,0:T(8,128)} custom-call(f32[1280,128]{1,0:T(8,128)} %shard_map.62.g_ref, f32[64,512]{1,0:T(8,128)} %bitcast.21), custom_call_target="tpu_custom_call" | custom-call | tf_op jit(solution)/shard_map/pallas_call | solution.py:242
  198.2 4.5 %convolution_bitcast_fusion = f32[8,1,64,256]{3,2,1,0:T(8,128)} fusion(f32[8,512,256]{2,1,0:T(8,128)} %get-tuple-element.6, f32[64,512]{1,0:T(8,128)} %shard_map.63), kind=kOutput, calls=%fused_computation | convolution fusion | flops 402653184 | bytes 4849664 | tf_op jit(solution)/shard_map/rzy,sz->rsy/dot_general | solution.py:370
